TPU v7x, 1024 devices: a whole 4x8x16 slice. The times are simulated.
1024 devices in a mesh: surf: 128 (over y, x, z_lo), depth: 8 (over z_hi, core).
Axes of the slice: x: 4, y: 8, z: 16 (z_hi: 4, z_lo: 4; z = z_hi * 4 + z_lo), core: 2. Of those that a mesh axis runs over, the one named last changes fastest.
Arguments:
- temp_old: float32 [64, 2048, 128], P('depth', 'surf'), may hold values from 0.5 to 2
- virgin: float32 [64, 2048, 128], P('depth', 'surf'), may hold values from 0.2 to 1
- zone: int32 [64, 2048, 128], P('depth', 'surf'), may hold values from 0 to 7, as said below
- zone_props: float32 [4, 8], replicated, as said below
- gas_flux: bfloat16 [16384, 128], P('surf'), may hold values from -6 to 6
- gas_owner: int32 [16384, 1], P('surf'), may hold values from 0 to 127; in each aligned block of 128 rows (0 to 127, 128 to 255, ...) at most 2 rows name the same one
- gas_cell: int32 [16384], P('surf'), may hold values from 0 to 15
Outputs:
- increment: float32 [64, 2048, 128], P('depth', 'surf')
Inputs may be any that keep to these rules, and one draw needn't show every extreme that they name: `gas_owner`: in the rows of one device at most 2 name the same owner. The zone is the same over aligned blocks of 8 cells through the thickness by 8 cells along the first surface dimension. `zone_props`: all entries positive.
All inputs are finite; a program needn't handle non-finite values.
Results may differ from a plain program's by a relative error of at most 0.0003.
Values may be sent and summed in bfloat16 or wider, within the bound.
A program may use at most 32 MiB of HBM per device.

v0:
```python
import jax
import jax.numpy as jnp
from jax import lax
from jax.sharding import PartitionSpec as P

LEVELS = 4
CYCLES = 2


omega_weight = 0.8


def extended(block, sides, width):
    for axis, dim in sides:
        count = lax.axis_size(axis)
        forward = [(i, i + 1) for i in range(count - 1)]
        backward = [(target, source) for source, target in forward]
        low = lax.ppermute(
            lax.slice_in_dim(block, block.shape[dim] - width, None, axis=dim), axis, forward
        )
        high = lax.ppermute(lax.slice_in_dim(block, 0, width, axis=dim), axis, backward)
        block = jnp.concatenate([low, block, high], axis=dim)
    return block


def weights_from_padded(padded_z, padded_x, cond_y, factor):
    faces_z = 0.5 * (padded_z[:-1] + padded_z[1:]) * factor
    faces_x = 0.5 * (padded_x[:, :-1] + padded_x[:, 1:]) * factor
    padded_y = jnp.pad(cond_y, ((0, 0), (0, 0), (1, 1)))
    faces_y = 0.5 * (padded_y[:, :, :-1] + padded_y[:, :, 1:])
    return (
        faces_z[:-1],
        faces_z[1:],
        faces_x[:, :-1],
        faces_x[:, 1:],
        faces_y[:, :, :-1],
        faces_y[:, :, 1:],
    )


def build_operator(diagonal, weights):
    lower_face, upper_face, west_face, east_face, south_face, north_face = weights
    centre = diagonal + lower_face + upper_face + west_face + east_face + south_face + north_face
    return (centre, lower_face, upper_face, west_face, east_face, south_face, north_face)


def operate(padded, operator):
    centre, lower_face, upper_face, west_face, east_face, south_face, north_face = operator
    middle = padded[1:-1, 1:-1]
    along_y = jnp.pad(middle, ((0, 0), (0, 0), (1, 1)))
    return (
        centre * middle
        - lower_face * padded[:-2, 1:-1]
        - upper_face * padded[2:, 1:-1]
        - west_face * padded[1:-1, :-2]
        - east_face * padded[1:-1, 2:]
        - south_face * along_y[:, :, :-2]
        - north_face * along_y[:, :, 2:]
    )


def restrict(field):
    depth_len, width_len, cross_len = field.shape
    return field.reshape(depth_len // 2, 2, width_len // 2, 2, cross_len).mean(axis=(1, 3))


def prolong(field):
    return jnp.repeat(jnp.repeat(field, 2, axis=0), 2, axis=1)


def line_solve(centre, lower_face, upper_face, rhs):
    zeros = jnp.zeros(rhs.shape[1:], jnp.float32)

    def forward(carry, rows):
        ratio_prev, value_prev = carry
        centre_row, lower_row, upper_row, rhs_row = rows
        denom = centre_row - lower_row * ratio_prev
        ratio = upper_row / denom
        value = (rhs_row + lower_row * value_prev) / denom
        return ((ratio, value), (ratio, value))

    unused, (ratios, values) = lax.scan(
        forward, (zeros, zeros), (centre, lower_face, upper_face, rhs)
    )

    def backward(later, rows):
        ratio, value = rows
        current = value + ratio * later
        return (current, current)

    unused_two, solved = lax.scan(backward, zeros, (ratios, values), reverse=True)
    return solved


def field_pad(field):
    return extended(field, (("surf", 1), ("depth", 0)), 1)


def vcycle(operators, coarse_parts, level, guess, rhs):
    operator = operators[level]
    if level == len(operators) - 1:
        column_rhs = lax.all_gather(rhs, "depth", axis=0, tiled=True)
        solved = line_solve(coarse_parts[0], coarse_parts[1], coarse_parts[2], column_rhs)
        own_rows = rhs.shape[0]
        return lax.dynamic_slice_in_dim(solved, lax.axis_index("depth") * own_rows, own_rows, 0)
    if guess is None:
        field = omega_weight * rhs / operator[0]
    else:
        field = guess + omega_weight * (rhs - operate(field_pad(guess), operator)) / operator[0]
    residual = rhs - operate(field_pad(field), operator)
    coarse = vcycle(operators, coarse_parts, level + 1, None, restrict(residual))
    field = field + prolong(coarse)
    return field + omega_weight * (rhs - operate(field_pad(field), operator)) / operator[0]


def wall_strip(gas_flux, gas_owner, gas_cell, width):
    flux_rows = lax.all_gather(gas_flux, "surf", axis=0, tiled=True)
    owner_rows = lax.all_gather(gas_owner, "surf", axis=0, tiled=True)
    cell_rows = lax.all_gather(gas_cell, "surf", axis=0, tiled=True)
    target = owner_rows[:, 0] * width + cell_rows
    mine = lax.axis_index("surf") * width + lax.iota(jnp.int32, width)
    placing = (mine[:, None] == target[None, :]).astype(jnp.bfloat16)
    return jnp.dot(placing, flux_rows, preferred_element_type=jnp.float32)


def per_device(temp_old, virgin, zone, zone_props, gas_flux, gas_owner, gas_cell):
    width = temp_old.shape[1]
    squared = temp_old * temp_old
    heat_factor = 0.5 + squared
    char_blend = 0.4 + 0.6 * virgin
    looked = [jnp.zeros_like(temp_old) for member in range(4)]
    for zone_index in range(zone_props.shape[1]):
        hit = zone == zone_index
        looked = [
            looked[member] + jnp.where(hit, zone_props[member, zone_index], 0.0)
            for member in range(4)
        ]
    cond_z = looked[0] * heat_factor * char_blend
    cond_x = looked[1] * heat_factor * char_blend
    cond_y = looked[2] * heat_factor * char_blend
    rate = 8.0 * virgin * jnp.exp(-3.0 / temp_old)
    diagonal = looked[3] * (0.5 + virgin) + 6.0 * rate / squared
    strip = wall_strip(gas_flux, gas_owner, gas_cell, width)
    on_top = lax.axis_index("depth") == 0
    source = (-2.0 * rate).at[0].add(jnp.where(on_top, strip, 0.0))
    fields = (diagonal, cond_z, cond_x, cond_y)
    operators = []
    for level in range(LEVELS):
        level_diag, level_z, level_x, level_y = fields
        stacked = jnp.stack([level_z, level_x])
        padded = extended(stacked, (("surf", 2), ("depth", 1)), 1)
        weights = weights_from_padded(padded[0][:, 1:-1], padded[1][1:-1], level_y, 0.25**level)
        operators.append(build_operator(level_diag, weights))
        if level < LEVELS - 1:
            fields = tuple((restrict(member) for member in fields))
    coarsest = operators[-1]
    coarse_parts = (
        lax.all_gather(coarsest[0], "depth", axis=0, tiled=True),
        lax.all_gather(coarsest[1], "depth", axis=0, tiled=True),
        lax.all_gather(coarsest[2], "depth", axis=0, tiled=True),
    )
    solution = None
    for cycle_index in range(CYCLES):
        solution = vcycle(operators, coarse_parts, 0, solution, source)
    return solution


def solution(mesh):
    return jax.shard_map(
        per_device,
        mesh=mesh,
        in_specs=(
            P("depth", "surf", None),
            P("depth", "surf", None),
            P("depth", "surf", None),
            P(),
            P("surf", None),
            P("surf", None),
            P("surf"),
        ),
        out_specs=P("depth", "surf", None),
        check_vma=False,
    )
```

profile of v0, /device:TPU:33, one launch (start us, length us, event | category | flops | bytes accessed | tf_op | source)
XLA Modules:
  0.0 1230.2 jit_solution(10152275564395039565)
XLA Ops:
  29.3 9.7 collective-permute-start.1
  41.0 9.4 collective-permute-start.9
  56.0 311.8 %all_gather.24 = s32[16384,1]{0,1:T(1,128)S(1)} all-gather(s32[128,1]{0,1:T(1,128)} %param.22), channel_id=1, replica_groups=mesh['surf'=128,'depth'=8] {'surf'}, dimensions={0}, use_global_device_ids=true | all-gather | bytes 66048 | tf_op jit(solution)/shard_map/all_gather | solution.py:118
  367.8 306.0 %all-gather.2 = s32[128,1,128]{2,1,0:T(1,128)S(1)} all-gather(s32[1,1,128]{2,1,0:T(1,128)} %bitcast.278), channel_id=1, replica_groups=mesh['surf'=128,'depth'=8] {'surf'}, dimensions={0}, use_global_device_ids=true | all-gather | bytes 66048 | tf_op jit(solution)/shard_map/all_gather | solution.py:119
  688.4 104.2 %collective-permute-start.23 = (f32[2,1,4,128]{3,2,1,0:T(4,128)S(1)}, f32[2,1,4,128]{3,2,1,0:T(4,128)S(1)}, u32[]{:S(2)}, u32[]{:S(2)}) collective-permute-start(f32[2,1,4,128]{3,2,1,0:T(4,128)S(1)} %pad_maximum_fusion.170), channel_id=1, source_target_pairs={{1,0},{2,1},{3,2},{4,3},{5,4},{6,5},{7,6},{9,8},{10,9},{11,10},{12... | collective-permute-start | bytes 12296 | tf_op jit(solution)/shard_map/ppermute | solution.py:21
  792.6 10.6 collective-permute-start.22
  805.2 7.5 collective-permute-start.18
  816.7 7.5 collective-permute-start.2
  840.7 7.2 collective-permute-done.4
  851.0 7.8 collective-permute-start.6
  874.1 9.3 collective-permute-start.14
  884.4 20.2 %all_gather.27 = f32[8,2,128]{2,1,0:T(2,128)S(1)} all-gather(f32[1,2,128]{2,1,0:T(2,128)S(1)} %get-tuple-element.589), channel_id=1, replica_groups=mesh['surf'=128,'depth'=8] {'depth'}, dimensions={0}, use_global_device_ids=true | all-gather | bytes 9216 | tf_op jit(solution)/shard_map/all_gather | solution.py:160
  909.9 12.8 %all_gather.28 = f32[8,2,128]{2,1,0:T(2,128)S(1)} all-gather(f32[1,2,128]{2,1,0:T(2,128)S(1)} %get-tuple-element.588), channel_id=1, replica_groups=mesh['surf'=128,'depth'=8] {'depth'}, dimensions={0}, use_global_device_ids=true | all-gather | bytes 9216 | tf_op jit(solution)/shard_map/all_gather | solution.py:158
  924.8 7.4 collective-permute-start.26
  932.2 12.7 %all_gather.29 = f32[8,2,128]{2,1,0:T(2,128)S(1)} all-gather(f32[1,2,128]{2,1,0:T(2,128)S(1)} %get-tuple-element.587), channel_id=1, replica_groups=mesh['surf'=128,'depth'=8] {'depth'}, dimensions={0}, use_global_device_ids=true | all-gather | bytes 9216 | tf_op jit(solution)/shard_map/all_gather | solution.py:159
  945.0 12.8 %all-gather.3 = f32[8,2,128]{2,1,0:T(2,128)S(1)} all-gather(f32[1,2,128]{2,1,0:T(2,128)S(1)} %multiply_bitcast_fusion.3), channel_id=2, replica_groups=mesh['surf'=128,'depth'=8] {'depth'}, dimensions={0}, use_global_device_ids=true | all-gather | bytes 9216 | tf_op jit(solution)/shard_map/all_gather | solution.py:102
  958.6 7.7 collective-permute-start.29
  968.2 8.4 collective-permute-done.28
  992.3 7.0 collective-permute-done.32
  1001.1 9.3 collective-permute-start.34
  1016.7 7.0 collective-permute-done.36
  1025.6 9.2 collective-permute-start.38
  1041.1 7.0 collective-permute-done.40
  1050.1 9.3 collective-permute-start.42
  1065.6 7.0 collective-permute-done.44
  1074.5 9.3 collective-permute-start.46
  1099.1 9.3 collective-permute-start.50
  1123.5 9.2 collective-permute-start.54
  1133.6 16.9 %all-gather.4 = f32[8,2,128]{2,1,0:T(2,128)S(1)} all-gather(f32[1,2,128]{2,1,0:T(2,128)S(1)} %multiply_bitcast_fusion.2), channel_id=3, replica_groups=mesh['surf'=128,'depth'=8] {'depth'}, dimensions={0}, use_global_device_ids=true | all-gather | bytes 9216 | tf_op jit(solution)/shard_map/all_gather | solution.py:102
  1188.0 9.3 collective-permute-start.62
  1203.6 7.0 collective-permute-done.64
  1212.5 9.2 collective-permute-start.66
  (301 shorter events, 217.0 us)
Async XLA Ops:
  6.5 820.6 %all-gather.7.cloned.1.call-start = ((), (), s32[]{:S(2)}) async-start(), calls=%async_computation | async-start | bytes 4227072 | tf_op jit(solution)/shard_map/all_gather | solution.py:117
  29.3 785.5 %collective-permute-start.1 = (f32[2,8,1,128]{3,2,1,0:T(1,128)S(1)}, f32[2,8,1,128]{3,2,1,0:T(1,128)S(1)}, u32[]{:S(2)}, u32[]{:S(2)}) collective-permute-start(f32[2,8,1,128]{3,2,1,0:T(1,128)S(1)} %get-tuple-element.512), channel_id=1, source_target_pairs={{8,0},{16,8},{24,16},{32,24},{40,32},{48,40},{56,48},{64,56},{72,6... | collective-permute-start | bytes 24584 | tf_op jit(solution)/shard_map/ppermute | solution.py:21
  39.0 775.8 %collective-permute-start = (f32[2,8,1,128]{3,2,1,0:T(1,128)S(1)}, f32[2,8,1,128]{3,2,1,0:T(1,128)S(1)}, u32[]{:S(2)}, u32[]{:S(2)}) collective-permute-start(f32[2,8,1,128]{3,2,1,0:T(1,128)S(1)} %get-tuple-element.511), channel_id=1, source_target_pairs={{0,8},{8,16},{16,24},{24,32},{32,40},{40,48},{48,56},{56,64},{64,7... | collective-permute-start | bytes 24584 | tf_op jit(solution)/shard_map/ppermute | solution.py:18
  41.0 751.6 %collective-permute-start.9 = (f32[2,4,1,128]{3,2,1,0:T(1,128)S(1)}, f32[2,4,1,128]{3,2,1,0:T(1,128)S(1)}, u32[]{:S(2)}, u32[]{:S(2)}) collective-permute-start(f32[2,4,1,128]{3,2,1,0:T(1,128)S(1)} %get-tuple-element.538), channel_id=1, source_target_pairs={{8,0},{16,8},{24,16},{32,24},{40,32},{48,40},{56,48},{64,56},{72,6... | collective-permute-start | bytes 12296 | tf_op jit(solution)/shard_map/ppermute | solution.py:21
  50.6 623.7 %collective-permute-start.21 = (f32[2,1,1,128]{3,2,1,0:T(1,128)S(1)}, f32[2,1,1,128]{3,2,1,0:T(1,128)S(1)}, u32[]{:S(2)}, u32[]{:S(2)}) collective-permute-start(f32[2,1,1,128]{3,2,1,0:T(1,128)S(1)} %get-tuple-element.591), channel_id=1, source_target_pairs={{8,0},{16,8},{24,16},{32,24},{40,32},{48,40},{56,48},{64,56},{72,6... | collective-permute-start | bytes 3080 | tf_op jit(solution)/shard_map/ppermute | solution.py:21
  52.5 625.5 %collective-permute-start.20 = (f32[2,1,1,128]{3,2,1,0:T(1,128)S(1)}, f32[2,1,1,128]{3,2,1,0:T(1,128)S(1)}, u32[]{:S(2)}, u32[]{:S(2)}) collective-permute-start(f32[2,1,1,128]{3,2,1,0:T(1,128)S(1)} %get-tuple-element.590), channel_id=1, source_target_pairs={{0,8},{8,16},{16,24},{24,32},{32,40},{40,48},{48,56},{56,64},{64,7... | collective-permute-start | bytes 3080 | tf_op jit(solution)/shard_map/ppermute | solution.py:18
  680.0 123.2 %collective-permute-start.8 = (f32[2,4,1,128]{3,2,1,0:T(1,128)S(1)}, f32[2,4,1,128]{3,2,1,0:T(1,128)S(1)}, u32[]{:S(2)}, u32[]{:S(2)}) collective-permute-start(f32[2,4,1,128]{3,2,1,0:T(1,128)S(1)} %get-tuple-element.537), channel_id=1, source_target_pairs={{0,8},{8,16},{16,24},{24,32},{32,40},{40,48},{48,56},{56,64},{64,7... | collective-permute-start | bytes 12296 | tf_op jit(solution)/shard_map/ppermute | solution.py:18
  688.4 116.8 %collective-permute-start.23 = (f32[2,1,4,128]{3,2,1,0:T(4,128)S(1)}, f32[2,1,4,128]{3,2,1,0:T(4,128)S(1)}, u32[]{:S(2)}, u32[]{:S(2)}) collective-permute-start(f32[2,1,4,128]{3,2,1,0:T(4,128)S(1)} %pad_maximum_fusion.170), channel_id=1, source_target_pairs={{1,0},{2,1},{3,2},{4,3},{5,4},{6,5},{7,6},{9,8},{10,9},{11,10},{12... | collective-permute-start | bytes 12296 | tf_op jit(solution)/shard_map/ppermute | solution.py:21
  792.6 20.2 %collective-permute-start.22 = (f32[2,1,4,128]{3,2,1,0:T(4,128)S(1)}, f32[2,1,4,128]{3,2,1,0:T(4,128)S(1)}, u32[]{:S(2)}, u32[]{:S(2)}) collective-permute-start(f32[2,1,4,128]{3,2,1,0:T(4,128)S(1)} %pad_maximum_fusion.170), channel_id=1, source_target_pairs={{0,1},{1,2},{2,3},{3,4},{4,5},{5,6},{6,7},{8,9},{9,10},{10,11},{11... | collective-permute-start | bytes 12296 | tf_op jit(solution)/shard_map/ppermute | solution.py:18
  803.2 62.0 %collective-permute-start.19 = (f32[2,1,6,128]{3,2,1,0:T(8,128)S(1)}, f32[2,1,6,128]{3,2,1,0:T(8,128)S(1)}, u32[]{:S(2)}, u32[]{:S(2)}) collective-permute-start(f32[2,1,6,128]{3,2,1,0:T(8,128)S(1)} %get-tuple-element.555), channel_id=1, source_target_pairs={{1,0},{2,1},{3,2},{4,3},{5,4},{6,5},{7,6},{9,8},{10,9},{11,10},{12... | collective-permute-start | bytes 18440 | tf_op jit(solution)/shard_map/ppermute | solution.py:21
  805.2 60.0 %collective-permute-start.18 = (f32[2,1,6,128]{3,2,1,0:T(8,128)S(1)}, f32[2,1,6,128]{3,2,1,0:T(8,128)S(1)}, u32[]{:S(2)}, u32[]{:S(2)}) collective-permute-start(f32[2,1,6,128]{3,2,1,0:T(8,128)S(1)} %get-tuple-element.554), channel_id=1, source_target_pairs={{0,1},{1,2},{2,3},{3,4},{4,5},{5,6},{6,7},{8,9},{9,10},{10,11},{11... | collective-permute-start | bytes 18440 | tf_op jit(solution)/shard_map/ppermute | solution.py:18
  812.8 24.7 %collective-permute-start.11 = (f32[2,1,10,128]{3,2,1,0:T(8,128)S(1)}, f32[2,1,10,128]{3,2,1,0:T(8,128)S(1)}, u32[]{:S(2)}, u32[]{:S(2)}) collective-permute-start(f32[2,1,10,128]{3,2,1,0:T(8,128)S(1)} %get-tuple-element.536), channel_id=1, source_target_pairs={{1,0},{2,1},{3,2},{4,3},{5,4},{6,5},{7,6},{9,8},{10,9},{11,10},{12... | collective-permute-start | bytes 30728 | tf_op jit(solution)/shard_map/ppermute | solution.py:21
  824.3 16.3 %collective-permute-start.10 = (f32[2,1,10,128]{3,2,1,0:T(8,128)S(1)}, f32[2,1,10,128]{3,2,1,0:T(8,128)S(1)}, u32[]{:S(2)}, u32[]{:S(2)}) collective-permute-start(f32[2,1,10,128]{3,2,1,0:T(8,128)S(1)} %get-tuple-element.535), channel_id=1, source_target_pairs={{0,1},{1,2},{2,3},{3,4},{4,5},{5,6},{6,7},{8,9},{9,10},{10,11},{11... | collective-permute-start | bytes 30728 | tf_op jit(solution)/shard_map/ppermute | solution.py:18
  837.5 10.4 collective-permute-start.4
  847.9 11.0 collective-permute-start.7
  872.2 11.2 collective-permute-start.15
  904.6 18.1 %collective-permute-start.25 = (f32[2,1,128]{2,1,0:T(1,128)S(1)}, f32[2,1,128]{2,1,0:T(1,128)S(1)}, u32[]{:S(2)}, u32[]{:S(2)}) collective-permute-start(f32[2,1,128]{2,1,0:T(1,128)S(1)} %get-tuple-element.579), channel_id=1, source_target_pairs={{8,0},{16,8},{24,16},{32,24},{40,32},{48,40},{56,48},{64,56},{72,6... | collective-permute-start | bytes 3080 | tf_op jit(solution)/shard_map/ppermute | solution.py:21
  906.5 16.2 %collective-permute-start.24 = (f32[2,1,128]{2,1,0:T(1,128)S(1)}, f32[2,1,128]{2,1,0:T(1,128)S(1)}, u32[]{:S(2)}, u32[]{:S(2)}) collective-permute-start(f32[2,1,128]{2,1,0:T(1,128)S(1)} %get-tuple-element.578), channel_id=1, source_target_pairs={{0,8},{8,16},{16,24},{24,32},{32,40},{40,48},{48,56},{56,64},{64,7... | collective-permute-start | bytes 3080 | tf_op jit(solution)/shard_map/ppermute | solution.py:18
  922.7 22.2 %collective-permute-start.27 = (f32[1,6,128]{2,1,0:T(8,128)S(1)}, f32[1,6,128]{2,1,0:T(8,128)S(1)}, u32[]{:S(2)}, u32[]{:S(2)}) collective-permute-start(f32[1,6,128]{2,1,0:T(8,128)S(1)} %get-tuple-element.569), channel_id=1, source_target_pairs={{1,0},{2,1},{3,2},{4,3},{5,4},{6,5},{7,6},{9,8},{10,9},{11,10},{12... | collective-permute-start | bytes 9224 | tf_op jit(solution)/shard_map/ppermute | solution.py:21
  924.8 20.1 %collective-permute-start.26 = (f32[1,6,128]{2,1,0:T(8,128)S(1)}, f32[1,6,128]{2,1,0:T(8,128)S(1)}, u32[]{:S(2)}, u32[]{:S(2)}) collective-permute-start(f32[1,6,128]{2,1,0:T(8,128)S(1)} %get-tuple-element.568), channel_id=1, source_target_pairs={{0,1},{1,2},{2,3},{3,4},{4,5},{5,6},{6,7},{8,9},{9,10},{10,11},{11... | collective-permute-start | bytes 9224 | tf_op jit(solution)/shard_map/ppermute | solution.py:18
  999.2 11.2 collective-permute-start.35
  1013.3 10.4 collective-permute-start.36
  1023.7 11.2 collective-permute-start.39
  1037.8 10.4 collective-permute-start.40
  1048.1 11.2 collective-permute-start.43
  1062.2 10.4 collective-permute-start.44
  1072.6 11.2 collective-permute-start.47
  1097.2 11.2 collective-permute-start.51
  1121.5 11.2 collective-permute-start.55
  1186.1 11.2 collective-permute-start.63
  1200.2 10.4 collective-permute-start.64
  1210.6 11.2 collective-permute-start.67
  (39 other events, 1933.7 us)
Sparse Core Ops, SparseCore 0:
  10.0 617.7 all-gather.6
where the time goes:
time: 1230 us
  blocking collectives  693 us (56%)
  starting transfers between devices  386 us (31%)
  waiting for transfers between devices  101 us (8%)
  other arithmetic  27.6 us (2%)
  between operations  15 us (1%)
    all_gather x1, blocking collectives, wall_strip(): owner_rows = lax.all_gather(gas_owner, 'surf', axis=0, tiled=True)  312 us
    all_gather x1, blocking collectives, wall_strip(): cell_rows = lax.all_gather(gas_cell, 'surf', axis=0, tiled=True)  306 us
    ppermute x34, starting transfers between devices, extended(): lax.ppermute(lax.slice_in_dim(block, 0, width, axis=dim), axis, backward)  195 us
    ppermute x34, starting transfers between devices, extended(): lax.ppermute(lax.slice_in_dim(block, block.shape[dim] - width, None, axis...  191 us
    ppermute x34, waiting for transfers between devices, extended(): lax.ppermute(lax.slice_in_dim(block, block.shape[dim] - width, None, axis...  100 us
    all_gather x2, blocking collectives, vcycle(): column_rhs = lax.all_gather(rhs, 'depth', axis=0, tiled=True)  29.7 us
  transfers between devices with their start and end apart: 69, of which 25 were waited for; matrix products, arithmetic and copies ran while one was open for 3% of the time, Pallas kernels for 0%

commit v1 on v0

v1 whole, which is shorter than its diff:
```python
import functools

import jax
import jax.numpy as jnp
from jax import lax
from jax.experimental import pallas as pl
from jax.experimental.pallas import tpu as pltpu
from jax.sharding import PartitionSpec as P

MESH = pl.DeviceIdType.MESH
F32 = jnp.float32
OMEGA = 0.8
LANES = 128
GROUP = 16


def roll(value, shift, axis):
    return pltpu.roll(value, shift % value.shape[axis], axis)


def gas_kernel(groups, width, span, flux_ref, target_ref, wall_ref,
               flux_all, target_all, partial, parts, send1, recv1, send2, recv2):
    surf, depth = lax.axis_index("surf"), lax.axis_index("depth")
    group, member = surf // span, lax.rem(surf, span)
    collects = (depth < 2) & (lax.rem(group, 2) == depth)
    owner = depth == 0
    halo = width // 2
    window = width + 2 * halo

    def source(other):
        return (other * span + member, depth)

    def summer(other):
        return (group * span + other, lax.rem(group, 2))

    def is_self(other):
        return owner & (lax.rem(group, 2) == 0) & (other == member)

    barrier = pltpu.get_barrier_semaphore()

    @pl.when(collects)
    def _():
        def greet(other, carry):
            @pl.when(other != group)
            def _():
                pl.semaphore_signal(barrier, inc=1, device_id=source(other), device_id_type=MESH)
            return carry
        lax.fori_loop(0, groups, greet, 0)

    @pl.when(owner)
    def _():
        def greet(other, carry):
            @pl.when(jnp.logical_not(is_self(other)))
            def _():
                pl.semaphore_signal(barrier, inc=1, device_id=summer(other), device_id_type=MESH)
            return carry
        lax.fori_loop(0, span, greet, 0)

    @pl.when(depth < 2)
    def _():
        pl.semaphore_wait(barrier, groups // 2 - jnp.where(collects, 1, 0)
                          + jnp.where(collects, span - jnp.where(depth == 0, 1, 0), 0))

    def copies1(to_group, slot):
        where = (to_group * span + member, depth)
        return (
            pltpu.make_async_remote_copy(
                src_ref=flux_ref, dst_ref=flux_all.at[slot], send_sem=send1.at[0, to_group],
                recv_sem=recv1.at[0, slot], device_id=where, device_id_type=MESH),
            pltpu.make_async_remote_copy(
                src_ref=target_ref, dst_ref=target_all.at[slot], send_sem=send1.at[1, to_group],
                recv_sem=recv1.at[1, slot], device_id=where, device_id_type=MESH),
        )

    def copy2(to_member, slot):
        return pltpu.make_async_remote_copy(
            src_ref=partial.at[pl.ds(pl.multiple_of(to_member * width, 8), window)],
            dst_ref=parts.at[slot], send_sem=send2.at[to_member], recv_sem=recv2.at[slot],
            device_id=(group * span + to_member, 0), device_id_type=MESH)

    @pl.when(depth < 2)
    def _():
        def push(half, carry):
            to_group = 2 * half + depth
            @pl.when(to_group != group)
            def _():
                for copy in copies1(to_group, group):
                    copy.start()
            return carry
        lax.fori_loop(0, groups // 2, push, 0)

    @pl.when(collects)
    def _():
        flux_all[group] = flux_ref[...]
        target_all[group] = target_ref[...]
        partial[...] = jnp.zeros_like(partial)
        rows = partial.shape[0]
        ids = group * (span * width) - halo + lax.broadcasted_iota(jnp.int32, (rows, LANES), 0)

        def add(other, carry):
            @pl.when(other != group)
            def _():
                for copy in copies1(other, other):
                    copy.wait_recv()
            placing = jnp.where(ids == target_all[other], 1.0, 0.0).astype(jnp.bfloat16)
            partial[...] += jnp.dot(placing, flux_all[other], preferred_element_type=F32)
            return carry
        lax.fori_loop(0, groups, add, 0)

        def push(to_member, carry):
            itself = is_self(to_member)
            @pl.when(itself)
            def _():
                parts[member] = partial[pl.ds(pl.multiple_of(member * width, 8), window)]
            @pl.when(jnp.logical_not(itself))
            def _():
                copy2(to_member, member).start()
            return carry
        lax.fori_loop(0, span, push, 0)

    wall_ref[...] = jnp.zeros_like(wall_ref)

    @pl.when(owner)
    def _():
        def add(other, carry):
            @pl.when(jnp.logical_not(is_self(other)))
            def _():
                copy2(other, other).wait_recv()
            wall_ref[...] += parts[other]
            return carry
        lax.fori_loop(0, span, add, 0)

    @pl.when(depth < 2)
    def _():
        def drain(half, carry):
            to_group = 2 * half + depth
            @pl.when(to_group != group)
            def _():
                for copy in copies1(to_group, group):
                    copy.wait_send()
            return carry
        lax.fori_loop(0, groups // 2, drain, 0)

    @pl.when(collects)
    def _():
        def drain(to_member, carry):
            @pl.when(jnp.logical_not(is_self(to_member)))
            def _():
                copy2(to_member, member).wait_send()
            return carry
        lax.fori_loop(0, span, drain, 0)


SIDES = [(dz, dx) for dz in (-1, 0, 1) for dx in (-1, 0, 1) if (dz, dx) != (0, 0)]


class Level:
    def __init__(self, refs, halo_z, halo_x):
        self.C, self.WX, self.WY, self.WI, self.B, self.WZ, self.U = refs
        self.rows, self.cols = self.C.shape[0], self.C.shape[1]
        self.halo_z, self.halo_x = halo_z, halo_x


def residual(level, field, first, count):
    here, up, down = (pl.ds(first + shift, count) for shift in (1, 2, 0))
    own = pl.ds(first, count)
    mid = field[here]
    wx, wy = level.WX[own], level.WY[own]
    total = level.B[own] - level.C[own] * mid
    total = total + level.WZ[here] * field[up] + level.WZ[down] * field[down]
    total = total + wx * roll(mid, -1, 1) + roll(wx * mid, 1, 1)
    return total + wy * roll(mid, -1, 2) + roll(wy * mid, 1, 2)


def restrict_into(source, skip, scratch, target, target_skip):
    rows, cols = scratch.shape[0], scratch.shape[1]
    for row in range(rows):
        scratch[row] = source[skip + 2 * row] + source[skip + 2 * row + 1]
    even = scratch[:, pl.ds(0, cols // 2, stride=2), :]
    odd = scratch[:, pl.ds(1, cols // 2, stride=2), :]
    target[pl.ds(target_skip, rows)] = 0.25 * (even + odd)


def prolong_onto(level, coarse, scratch, first, count):
    cols = scratch.shape[1]
    low, number = first // 2, count // 2
    part = coarse[pl.ds(low, number)]
    scratch[pl.ds(low, number), pl.ds(0, cols // 2, stride=2), :] = part
    scratch[pl.ds(low, number), pl.ds(1, cols // 2, stride=2), :] = part
    for row in range(low, low + number):
        wide = scratch[row]
        level.U[1 + 2 * row] = level.U[1 + 2 * row] + wide
        level.U[2 + 2 * row] = level.U[2 + 2 * row] + wide


def cycles_kernel(n_surf, n_depth, n_zones,
                  temp_ref, virgin_ref, zone_ref, props_ref, wall_ref, out_ref,
                  packed, guess, temp, virgin,
                  fd0, fx0, fy0, fz0, fd1, fx1, fy1, fz1, fd2, fx2, fy2, fz2, fd3, fx3, fy3, fz3,
                  l0, l1, l2, res, t0, t1, t2, v1, v2, b3,
                  coef_own, coef_all, rhs_own, rhs_all, ratio, inverse, solved, e2,
                  z_out, z_in, x_out, x_in,
                  s_send, s_recv, e_send, e_recv, g_send, g_recv, h_send, h_recv):
    surf, depth = lax.axis_index("surf"), lax.axis_index("depth")

    def at(dz, dx):
        return (lax.rem(surf + dx + n_surf, n_surf), lax.rem(depth + dz + n_depth, n_depth))

    levels = [Level(refs, 8 >> index, 8 >> index) for index, refs in enumerate((l0, l1, l2))]
    top, mid, low = levels

    barrier = pltpu.get_barrier_semaphore()

    def greet(dz, carry):
        for dx in (-1, 0, 1):
            pl.semaphore_signal(barrier, inc=1, device_id=at(dz, dx), device_id_type=MESH)
        return carry

    for dx in (-1, 1):
        pl.semaphore_signal(barrier, inc=1, device_id=at(0, dx), device_id_type=MESH)
    lax.fori_loop(1, n_depth, greet, 0)

    own_t = temp_ref[...]
    own_v = virgin_ref[...]
    code_t = ((own_t - 0.5) * (65535.0 / 1.5) + 0.5).astype(jnp.int32)
    code_v = ((own_v - 0.2) * (65535.0 / 0.8) + 0.5).astype(jnp.int32)
    packed[1, 0:8, 8:24] = jnp.left_shift(code_t, 16) | code_v
    packed[1, 8, 8:24] = zone_ref[0]
    pl.semaphore_wait(barrier, 3 * n_depth - 1)

    src_x = {-1: (8, 8), 0: (8, 16), 1: (16, 8)}
    dst_x = {-1: 24, 0: 8, 1: 0}

    def ring_copy(index, ref_src, ref_dst, send, recv, dz, dx):
        return pltpu.make_async_remote_copy(
            src_ref=ref_src, dst_ref=ref_dst, send_sem=send.at[index], recv_sem=recv.at[index],
            device_id=at(dz, dx), device_id_type=MESH)

    def setup_copy(index):
        dz, dx = SIDES[index]
        first, count = src_x[dx]
        return ring_copy(
            index, packed.at[1, :, pl.ds(first, count)],
            packed.at[1 - dz, :, pl.ds(dst_x[dx], count)], s_send, s_recv, dz, dx)

    def guess_copy(index):
        dz, dx = SIDES[index]
        first, count = src_x[dx]
        low_row, rows = (0, 8) if dx == 0 or dz == 0 else ((0, 7) if dz < 0 else (1, 7))
        return ring_copy(
            index, guess.at[pl.ds(9 + low_row, rows), pl.ds(first, count)],
            guess.at[pl.ds(1 + 8 * (1 - dz) + low_row, rows), pl.ds(dst_x[dx], count)],
            e_send, e_recv, dz, dx)

    for index in range(8):
        setup_copy(index).start()

    def column_mask(level):
        column = lax.broadcasted_iota(jnp.int32, (level.cols, LANES), 0)
        first, last = level.halo_x, level.cols - level.halo_x
        inside = ((column >= first) | (surf > 0)) & ((column < last) | (surf < n_surf - 1))
        return jnp.where(inside, 1.0, 0.0)

    row_mask = [jnp.where(depth > 0, 1.0, 0.0), jnp.float32(1.0), jnp.where(depth < n_depth - 1, 1.0, 0.0)]
    masks = [column_mask(level) for level in levels]
    for level in levels:
        zero = jnp.zeros((level.cols, LANES), F32)
        level.WZ[0] = zero
        level.U[0] = zero
        level.U[level.rows + 1] = zero
    for ref in (fz0, fz1, fz2):
        ref[0] = jnp.zeros(ref.shape[1:], F32)
        ref[ref.shape[0] - 1] = jnp.zeros(ref.shape[1:], F32)
    guess[0] = jnp.zeros(guess.shape[1:], F32)
    guess[25] = jnp.zeros(guess.shape[1:], F32)
    solved[0] = jnp.zeros(solved.shape[1:], F32)
    solved[n_depth + 1] = jnp.zeros(solved.shape[1:], F32)

    for index in range(8):
        setup_copy(index).wait_recv()
    for block in range(3):
        code = packed[block, 0:8]
        rows = pl.ds(8 * block, 8)
        temp[rows] = 0.5 + lax.shift_right_logical(code, 16).astype(F32) * (1.5 / 65535.0)
        virgin[rows] = 0.2 + (code & 0xFFFF).astype(F32) * (0.8 / 65535.0)
    temp[8:16, 8:24] = own_t
    virgin[8:16, 8:24] = own_v
    for block in range(3):
        zone = packed[block, 8]
        inside = masks[0] * row_mask[block]
        props = [jnp.zeros((top.cols, LANES), F32) for _ in range(4)]
        for number in range(n_zones):
            hit = zone == number
            props = [jnp.where(hit, props_ref[kind, number], props[kind]) for kind in range(4)]
        props = [value * inside for value in props]
        for row in range(8 * block, 8 * block + 8, 2):
            rows = pl.ds(row, 2)
            t, v = temp[rows], virgin[rows]
            squared = t * t
            blend = (0.5 + squared) * (0.4 + 0.6 * v)
            rate = 8.0 * v * jnp.exp(-3.0 / t)
            fz0[pl.ds(row + 1, 2)] = props[0] * blend
            fx0[rows] = props[1] * blend
            fy0[rows] = props[2] * blend
            fd0[rows] = (props[3] * (0.5 + v) + 6.0 * rate / squared) * inside
            top.B[rows] = -2.0 * rate * inside

    fields = [(fd0, fx0, fy0, fz0), (fd1, fx1, fy1, fz1), (fd2, fx2, fy2, fz2), (fd3, fx3, fy3, fz3)]
    scratches = (t0, t1, t2)

    for index, level in enumerate(levels):
        fd, fx, fy, fz = fields[index]
        half = 0.5 * 0.25**index
        step = min(4, level.halo_z)
        lane = lax.broadcasted_iota(jnp.int32, (step, level.cols, LANES), 2)
        for row in range(0, level.rows, step):
            rows = pl.ds(row, step)
            inside = masks[index] * row_mask[row // level.halo_z]
            here = fz[pl.ds(row + 1, step)]
            lower = half * (here + fz[rows])
            upper = half * (here + fz[pl.ds(row + 2, step)])
            level.WZ[pl.ds(row + 1, step)] = upper
            across = fx[rows]
            east = half * (across + roll(across, -1, 1))
            west = roll(east, 1, 1)
            level.WX[rows] = east
            along = fy[rows]
            north = 0.5 * (along + jnp.where(lane == LANES - 1, 0.0, roll(along, -1, 2)))
            south = 0.5 * (along + jnp.where(lane == 0, 0.0, roll(along, 1, 2)))
            level.WY[rows] = jnp.where(lane == LANES - 1, 0.0, north)
            centre = fd[rows] + lower + upper + west + east + south + north
            level.C[rows] = centre
            level.WI[rows] = jnp.where((inside > 0.0)[None], OMEGA / centre, 0.0)
        for kind in range(4):
            skip = 1 if kind == 3 else 0
            target_skip = 1 if kind == 3 and index < 2 else 0
            restrict_into(fields[index][kind], skip, scratches[index], fields[index + 1][kind], target_skip)

    half = 0.5 * 0.25**3
    centre_z, centre_x, centre_y = fz3[1, 1:3], fx3[1, 1:3], fy3[1, 1:3]
    lane = lax.broadcasted_iota(jnp.int32, (2, LANES), 1)
    lower = half * (centre_z + fz3[0, 1:3])
    upper = half * (centre_z + fz3[2, 1:3])
    west = half * (centre_x + fx3[1, 0:2])
    east = half * (centre_x + fx3[1, 2:4])
    north = 0.5 * (centre_y + jnp.where(lane == LANES - 1, 0.0, roll(centre_y, -1, 1)))
    south = 0.5 * (centre_y + jnp.where(lane == 0, 0.0, roll(centre_y, 1, 1)))
    centre = fd3[1, 1:3] + lower + upper + west + east + south + north
    for column in range(2):
        coef_own[0, column] = centre[column : column + 1]
        coef_own[1, column] = upper[column : column + 1]

    source_column = {-1: (0, 1), 0: (0, 2), 1: (1, 1)}
    landing_column = {-1: 3, 0: 1, 1: 0}

    def column_copy(phase, dz, dx):
        first, count = source_column[dx]
        if phase == 0:
            src, dst = coef_own.at[:, pl.ds(first, count)], coef_all.at[depth, :, pl.ds(landing_column[dx], count)]
        else:
            src = rhs_own.at[phase - 1, pl.ds(first, count)]
            dst = rhs_all.at[phase - 1, depth, pl.ds(landing_column[dx], count)]
        return pltpu.make_async_remote_copy(
            src_ref=src, dst_ref=dst, send_sem=g_send.at[phase, dz, dx + 1],
            recv_sem=g_recv.at[phase, dz, dx + 1], device_id=at(dz, dx), device_id_type=MESH)

    def each_column(phase, act):
        for dx in (-1, 1):
            act(column_copy(phase, 0, dx))

        def body(dz, carry):
            for dx in (-1, 0, 1):
                act(column_copy(phase, dz, dx))
            return carry

        lax.fori_loop(1, n_depth, body, 0)

    each_column(0, lambda copy: copy.start())
    coef_all[depth, :, 1:3] = coef_own[...]

    @pl.when(depth == 0)
    def _():
        top.B[8] = top.B[8] + wall_ref[...]

    def down(level, scratch, coarse_rhs, chunk):
        for row in range(0, level.rows, chunk):
            res[pl.ds(row, chunk), 0 : level.cols] = residual(level, level.U, row, chunk)
        restrict_into(res.at[:, pl.ds(0, level.cols)], 0, scratch, coarse_rhs, 0)

    def near_copies(cycle):
        pairs = []
        for index, (dz, dx) in enumerate(((-1, 0), (1, 0), (0, -1), (0, 1))):
            side = index % 2
            out, into = (z_out, z_in) if dz else (x_out, x_in)
            pairs.append(pltpu.make_async_remote_copy(
                src_ref=out.at[cycle, side], dst_ref=into.at[cycle, 1 - side],
                send_sem=h_send.at[cycle, index], recv_sem=h_recv.at[cycle, index],
                device_id=at(dz, dx), device_id_type=MESH))
        return pairs

    def run_cycle(cycle, last):
        down(top, t0, mid.B, 4)
        mid.U[1:13] = mid.WI[...] * mid.B[...]
        down(mid, t1, low.B, 4)
        low.U[1:7] = low.WI[...] * low.B[...]
        down(low, t2, b3, 6)
        for column in range(2):
            rhs_own[cycle, column] = b3[1, 1 + column : 2 + column]
        each_column(1 + cycle, lambda copy: copy.start())
        z_out[cycle, 0, 0] = low.B[2]
        z_out[cycle, 0, 1] = low.U[4]
        z_out[cycle, 1, 0] = low.B[3]
        z_out[cycle, 1, 1] = low.U[3]
        for row in range(4):
            x_out[cycle, 0, row] = low.U[2 + row, 3:4]
            x_out[cycle, 1, row] = low.U[2 + row, 4:5]
        near = near_copies(cycle)
        for copy in near:
            copy.start()
        rhs_all[cycle, depth, 1:3] = rhs_own[cycle]

        if cycle == 0:
            each_column(0, lambda copy: copy.wait_recv())
            inv = 1.0 / coef_all[0, 0]
            inverse[0] = inv
            ratio[0] = coef_all[0, 1] * inv
            for row in range(1, n_depth):
                inv = 1.0 / (coef_all[row, 0] - coef_all[row - 1, 1] * ratio[row - 1])
                inverse[row] = inv
                ratio[row] = coef_all[row, 1] * inv

        for copy in near:
            copy.wait_recv()
        low.B[1] = z_in[cycle, 0, 0]
        low.B[4] = z_in[cycle, 1, 0]
        low.U[2] = low.WI[1] * low.B[1]
        low.U[5] = low.WI[4] * low.B[4]
        low.U[1] = z_in[cycle, 0, 1] * (masks[2] * row_mask[0])
        low.U[6] = z_in[cycle, 1, 1] * (masks[2] * row_mask[2])
        for row in range(4):
            block = (0, 1, 1, 2)[row]
            first = jnp.where(surf > 0, 1.0, 0.0) * row_mask[block]
            final = jnp.where(surf < n_surf - 1, 1.0, 0.0) * row_mask[block]
            low.U[2 + row, 0:1] = x_in[cycle, 0, row] * first
            low.U[2 + row, 7:8] = x_in[cycle, 1, row] * final

        each_column(1 + cycle, lambda copy: copy.wait_recv())
        value = rhs_all[cycle, 0] * inverse[0]
        values = [value]
        for row in range(1, n_depth):
            value = (rhs_all[cycle, row] + coef_all[row - 1, 1] * value) * inverse[row]
            values.append(value)
        later = values[-1]
        solved[n_depth] = later
        for row in range(n_depth - 2, -1, -1):
            later = values[row] + ratio[row] * later
            solved[row + 1] = later
        for row in range(3):
            for column in range(4):
                value = solved[depth + row, column]
                if column == 0:
                    value = value * jnp.where(surf > 0, 1.0, 0.0)
                if column == 3:
                    value = value * jnp.where(surf < n_surf - 1, 1.0, 0.0)
                e2[row, 2 * column : 2 * column + 2] = jnp.broadcast_to(value, (2, LANES))
        for row in range(3):
            wide = e2[row]
            low.U[1 + 2 * row] = low.U[1 + 2 * row] + wide
            low.U[2 + 2 * row] = low.U[2 + 2 * row] + wide
        v2[...] = low.U[1:7] + low.WI[...] * residual(low, low.U, 0, 6)
        prolong_onto(mid, v2, t1, 2, 8)
        v1[2:10] = mid.U[3:11] + mid.WI[2:10] * residual(mid, mid.U, 2, 8)
        prolong_onto(top, v1, t0, 6, 12)
        for row in range(8, 16, 4):
            rows = pl.ds(row, 4)
            new = top.U[pl.ds(row + 1, 4)] + top.WI[rows] * residual(top, top.U, row, 4)
            if last:
                out_ref[pl.ds(row - 8, 4)] = new[:, 8:24]
            else:
                guess[pl.ds(row + 1, 4), 8:24] = new[:, 8:24]

    top.U[1:25] = top.WI[...] * top.B[...]
    run_cycle(0, False)
    for index in range(8):
        guess_copy(index).start()
    for index in range(8):
        guess_copy(index).wait_recv()
    for rows in (pl.ds(1, 1), pl.ds(24, 1)):
        for columns in (pl.ds(0, 8), pl.ds(24, 8)):
            guess[rows, columns] = jnp.zeros((1, 8, LANES), F32)
    for block in range(3):
        rows = pl.ds(1 + 8 * block, 8)
        if block == 1:
            for columns, inside in ((slice(0, 8), surf > 0), (slice(24, 32), surf < n_surf - 1)):
                guess[rows, columns] = guess[rows, columns] * jnp.where(inside, 1.0, 0.0)
        else:
            guess[rows] = guess[rows] * (masks[0] * row_mask[block])
    for row in range(0, 24, 4):
        rows, padded = pl.ds(row, 4), pl.ds(row + 1, 4)
        top.U[padded] = guess[padded] + top.WI[rows] * residual(top, guess, row, 4)
    run_cycle(1, True)

    for index in range(8):
        setup_copy(index).wait_send()
        guess_copy(index).wait_send()
    for phase in range(3):
        each_column(phase, lambda copy: copy.wait_send())
    for cycle in range(2):
        for copy in near_copies(cycle):
            copy.wait_send()


def per_device(n_surf, n_depth, temp_old, virgin, zone, zone_props, gas_flux, gas_owner, gas_cell):
    width = temp_old.shape[1]
    span = min(GROUP, n_surf // 2)
    groups = n_surf // span
    vmem = pl.BlockSpec(memory_space=pltpu.VMEM)
    smem = pl.BlockSpec(memory_space=pltpu.SMEM)
    dma = pltpu.SemaphoreType.DMA
    rows = gas_flux.shape[0]
    target = (gas_owner[:, 0] * width + gas_cell).reshape(1, rows)

    wall = pl.pallas_call(
        functools.partial(gas_kernel, groups, width, span),
        out_shape=jax.ShapeDtypeStruct((2 * width, LANES), F32),
        in_specs=[vmem, vmem],
        out_specs=vmem,
        scratch_shapes=[
            pltpu.VMEM((groups, rows, LANES), jnp.bfloat16),
            pltpu.VMEM((groups, 1, rows), jnp.int32),
            pltpu.VMEM((span * width + width, LANES), F32),
            pltpu.VMEM((span, 2 * width, LANES), F32),
            dma((2, groups)), dma((2, groups)), dma((span,)), dma((span,)),
        ],
        compiler_params=pltpu.CompilerParams(collective_id=0, has_side_effects=True),
        name="wall",
    )(gas_flux, target)

    def box(*shape):
        return pltpu.VMEM((*shape, LANES), F32)

    def fields(index):
        r, c = 24 >> index, 32 >> index
        return [box(r, c), box(r, c), box(r, c), box(r if index == 3 else r + 2, c)]

    def level(index):
        r, c = 24 >> index, 32 >> index
        return [box(r, c)] * 5 + [box(r + 2, c)] * 2

    scratch = [
        pltpu.VMEM((3, 9, 32, LANES), jnp.int32), box(26, 32), box(24, 32), box(24, 32),
        *fields(0), *fields(1), *fields(2), *fields(3),
        level(0), level(1), level(2),
        box(24, 32), box(12, 32), box(6, 16), box(3, 8), box(12, 16), box(6, 8), box(3, 4),
        box(2, 2, 1), box(n_depth, 2, 4, 1), box(2, 2, 1), box(2, n_depth, 4, 1),
        box(n_depth, 4, 1), box(n_depth, 4, 1), box(n_depth + 2, 4, 1), box(3, 8),
        box(2, 2, 2, 8), box(2, 2, 2, 8), box(2, 2, 4, 1), box(2, 2, 4, 1),
        dma((8,)), dma((8,)), dma((8,)), dma((8,)),
        dma((3, n_depth, 3)), dma((3, n_depth, 3)), dma((2, 4)), dma((2, 4)),
    ]
    return pl.pallas_call(
        functools.partial(cycles_kernel, n_surf, n_depth, zone_props.shape[1]),
        out_shape=jax.ShapeDtypeStruct(temp_old.shape, F32),
        in_specs=[vmem, vmem, vmem, smem, vmem],
        out_specs=vmem,
        scratch_shapes=scratch,
        compiler_params=pltpu.CompilerParams(
            collective_id=1, has_side_effects=True, vmem_limit_bytes=48 * 1024 * 1024),
        name="cycles",
    )(temp_old, virgin, zone, zone_props, wall)


def solution(mesh):
    return jax.shard_map(
        functools.partial(per_device, mesh.shape["surf"], mesh.shape["depth"]),
        mesh=mesh,
        in_specs=(
            P("depth", "surf", None),
            P("depth", "surf", None),
            P("depth", "surf", None),
            P(),
            P("surf", None),
            P("surf", None),
            P("surf"),
        ),
        out_specs=P("depth", "surf", None),
        check_vma=False,
    )
```

time: 1230 us -> 87.3 us (0.07)
  the two profiles are of different devices: /device:TPU:33 before, /device:TPU:9 now
where the time goes in v1:
time: 87.3 us; the launch traced here: 86.9 us
  Pallas kernels  81.8 us (94%)
  local copies, waits for them, and re-layouts  3.87 us (4%)
  other arithmetic  1.18 us (1%)
    pallas_call x1, Pallas kernels, per_device(): pl.pallas_call(functools.partial(cycles_kernel, n_surf, n_depth, zone_pro...  60.8 us
    pallas_call x1, Pallas kernels, per_device(): pl.pallas_call(functools.partial(gas_kernel, groups, width, span), out_sh...  21 us
    unnamed x11, local copies, waits for them, and re-layouts  3.87 us

profile of v1, /device:TPU:9, one launch (start us, length us, event | category | flops | bytes accessed | tf_op | source)
XLA Modules:
  0.0 86.9 jit_solution(2742315840881617749)
XLA Ops:
  0.0 1.2 %fusion.target_ref = s32[1,128]{1,0:T(1,128)} fusion(s32[128]{0:T(128)} %param.13, s32[128,1]{0,1:T(1,128)} %param.12), kind=kLoop, calls=%fused_computation.1 | loop fusion | flops 256 | bytes 1536 | tf_op jit(solution)/shard_map/reshape | solution.py:521
  1.2 0.0 copy-start.4
  1.2 21.0 %wall.1.wall_ref = f32[32,128]{1,0:T(8,128)} custom-call(bf16[128,128]{1,0:T(8,128)(2,1)} %flux_ref.1, s32[1,128]{1,0:T(1,128)} %fusion.target_ref), custom_call_target="tpu_custom_call" | custom-call | tf_op jit(solution)/shard_map/wall/pallas_call | solution.py:523
  22.2 0.0 copy-done.4
  22.2 0.0 copy-start
  22.2 0.8 copy-done
  23.1 0.0 copy-start.1
  23.1 0.8 copy-done.1
  23.9 0.0 copy-start.2
  23.9 0.8 copy-done.2
  24.7 0.0 copy-start.3
  24.7 0.7 copy-done.3
  25.5 60.8 %cycles.1 = f32[8,16,128]{2,1,0:T(8,128)S(1)} custom-call(f32[8,16,128]{2,1,0:T(8,128)S(1)} %copy-done, f32[8,16,128]{2,1,0:T(8,128)S(1)} %copy-done.1, s32[8,16,128]{2,1,0:T(8,128)S(1)} %copy-done.2, f32[4,8]{1,0:T(4,128)S(1)} %copy-done.4, f32[32,128]{1,0:T(8,128)S(1)} %copy-done.3), custom_call_target="tpu_custom_call" | custom-call | tf_op jit(solution)/shard_map/cycles/pallas_call | solution.py:561
  86.2 0.6 copy.9
Async XLA Ops:
  1.2 21.0 %copy-start.4 = (f32[4,8]{1,0:T(4,128)S(1)}, f32[4,8]{1,0:T(4,128)}, u32[]{:S(2)}) copy-start(f32[4,8]{1,0:T(4,128)} %props_ref.1) | copy-start | bytes 388
  22.2 0.8 copy-start
  23.1 0.8 copy-start.1
  23.9 0.8 copy-start.2
  24.7 0.7 copy-start.3

commit v2 on v1

--- a/solution.py
+++ b/solution.py
@@ -18,137 +18,126 @@
     return pltpu.roll(value, shift % value.shape[axis], axis)
 
 
-def gas_kernel(groups, width, span, flux_ref, target_ref, wall_ref,
-               flux_all, target_all, partial, parts, send1, recv1, send2, recv2):
-    surf, depth = lax.axis_index("surf"), lax.axis_index("depth")
-    group, member = surf // span, lax.rem(surf, span)
-    collects = (depth < 2) & (lax.rem(group, 2) == depth)
-    owner = depth == 0
-    halo = width // 2
-    window = width + 2 * halo
-
-    def source(other):
-        return (other * span + member, depth)
-
-    def summer(other):
-        return (group * span + other, lax.rem(group, 2))
-
-    def is_self(other):
-        return owner & (lax.rem(group, 2) == 0) & (other == member)
-
-    barrier = pltpu.get_barrier_semaphore()
-
-    @pl.when(collects)
-    def _():
-        def greet(other, carry):
-            @pl.when(other != group)
+class Wall:
+    def __init__(self, groups, span, width, refs):
+        (self.flux, self.target, self.flux_all, self.target_all, self.partial, self.parts,
+         self.send1, self.recv1, self.send2, self.recv2) = refs
+        self.groups, self.span, self.width = groups, span, width
+        surf, self.depth = lax.axis_index("surf"), lax.axis_index("depth")
+        self.group, self.member = surf // span, lax.rem(surf, span)
+        self.collects = (self.depth < 2) & (lax.rem(self.group, 2) == self.depth)
+        self.owner = self.depth == 0
+
+    def is_self(self, other):
+        return self.owner & (lax.rem(self.group, 2) == 0) & (other == self.member)
+
+    def copies1(self, to_group, slot):
+        where = (to_group * self.span + self.member, self.depth)
+        return [
+            pltpu.make_async_remote_copy(
+                src_ref=src, dst_ref=dst.at[slot], send_sem=self.send1.at[kind, to_group],
+                recv_sem=self.recv1.at[kind, slot], device_id=where, device_id_type=MESH)
+            for kind, (src, dst) in enumerate(((self.flux, self.flux_all), (self.target, self.target_all)))
+        ]
+
+    def rows_for(self, member):
+        return self.partial.at[pl.ds(pl.multiple_of(member * self.width, 8), 2 * self.width)]
+
+    def copy2(self, to_member, slot):
+        return pltpu.make_async_remote_copy(
+            src_ref=self.rows_for(to_member), dst_ref=self.parts.at[slot],
+            send_sem=self.send2.at[to_member], recv_sem=self.recv2.at[slot],
+            device_id=(self.group * self.span + to_member, 0), device_id_type=MESH)
+
+    def greet(self, barrier):
+        @pl.when(self.collects)
+        def _():
+            def body(other, carry):
+                @pl.when(other != self.group)
+                def _():
+                    pl.semaphore_signal(
+                        barrier, inc=1, device_id=(other * self.span + self.member, self.depth), device_id_type=MESH)
+                return carry
+            lax.fori_loop(0, self.groups, body, 0)
+
+        @pl.when(self.owner)
+        def _():
+            def body(other, carry):
+                @pl.when(jnp.logical_not(self.is_self(other)))
+                def _():
+                    pl.semaphore_signal(
+                        barrier, inc=1, device_id=(self.group * self.span + other, lax.rem(self.group, 2)),
+                        device_id_type=MESH)
+                return carry
+            lax.fori_loop(0, self.span, body, 0)
+
+    def greetings(self):
+        collecting = jnp.where(self.collects, 1, 0)
+        from_owners = collecting * (self.span - jnp.where(self.owner, 1, 0))
+        return jnp.where(self.depth < 2, self.groups // 2 - collecting, 0) + from_owners
+
+    def each_group(self, act):
+        @pl.when(self.depth < 2)
+        def _():
+            def body(half, carry):
+                to_group = 2 * half + self.depth
+                @pl.when(to_group != self.group)
+                def _():
+                    for copy in self.copies1(to_group, self.group):
+                        act(copy)
+                return carry
+            lax.fori_loop(0, self.groups // 2, body, 0)
+
+    def each_member(self, act):
+        def body(member, carry):
+            @pl.when(jnp.logical_not(self.is_self(member)))
             def _():
-                pl.semaphore_signal(barrier, inc=1, device_id=source(other), device_id_type=MESH)
+                act(self.copy2(member, self.member))
             return carry
-        lax.fori_loop(0, groups, greet, 0)
-
-    @pl.when(owner)
-    def _():
-        def greet(other, carry):
-            @pl.when(jnp.logical_not(is_self(other)))
+        lax.fori_loop(0, self.span, body, 0)
+
+    def collect(self):
+        @pl.when(self.collects)
+        def _():
+            self.flux_all[self.group] = self.flux[...]
+            self.target_all[self.group] = self.target[...]
+            self.partial[...] = jnp.zeros_like(self.partial)
+            rows = self.partial.shape[0]
+            first = self.group * (self.span * self.width) - self.width // 2
+            ids = first + lax.broadcasted_iota(jnp.int32, (rows, LANES), 0)
+
+            def add(other, carry):
+                @pl.when(other != self.group)
+                def _():
+                    for copy in self.copies1(other, other):
+                        copy.wait_recv()
+                placing = jnp.where(ids == self.target_all[other], 1.0, 0.0).astype(jnp.bfloat16)
+                self.partial[...] += jnp.dot(placing, self.flux_all[other], preferred_element_type=F32)
+                return carry
+            lax.fori_loop(0, self.groups, add, 0)
+
+            @pl.when(self.is_self(self.member))
             def _():
-                pl.semaphore_signal(barrier, inc=1, device_id=summer(other), device_id_type=MESH)
-            return carry
-        lax.fori_loop(0, span, greet, 0)
-
-    @pl.when(depth < 2)
-    def _():
-        pl.semaphore_wait(barrier, groups // 2 - jnp.where(collects, 1, 0)
-                          + jnp.where(collects, span - jnp.where(depth == 0, 1, 0), 0))
-
-    def copies1(to_group, slot):
-        where = (to_group * span + member, depth)
-        return (
-            pltpu.make_async_remote_copy(
-                src_ref=flux_ref, dst_ref=flux_all.at[slot], send_sem=send1.at[0, to_group],
-                recv_sem=recv1.at[0, slot], device_id=where, device_id_type=MESH),
-            pltpu.make_async_remote_copy(
-                src_ref=target_ref, dst_ref=target_all.at[slot], send_sem=send1.at[1, to_group],
-                recv_sem=recv1.at[1, slot], device_id=where, device_id_type=MESH),
-        )
-
-    def copy2(to_member, slot):
-        return pltpu.make_async_remote_copy(
-            src_ref=partial.at[pl.ds(pl.multiple_of(to_member * width, 8), window)],
-            dst_ref=parts.at[slot], send_sem=send2.at[to_member], recv_sem=recv2.at[slot],
-            device_id=(group * span + to_member, 0), device_id_type=MESH)
-
-    @pl.when(depth < 2)
-    def _():
-        def push(half, carry):
-            to_group = 2 * half + depth
-            @pl.when(to_group != group)
-            def _():
-                for copy in copies1(to_group, group):
-                    copy.start()
-            return carry
-        lax.fori_loop(0, groups // 2, push, 0)
-
-    @pl.when(collects)
-    def _():
-        flux_all[group] = flux_ref[...]
-        target_all[group] = target_ref[...]
-        partial[...] = jnp.zeros_like(partial)
-        rows = partial.shape[0]
-        ids = group * (span * width) - halo + lax.broadcasted_iota(jnp.int32, (rows, LANES), 0)
-
-        def add(other, carry):
-            @pl.when(other != group)
-            def _():
-                for copy in copies1(other, other):
-                    copy.wait_recv()
-            placing = jnp.where(ids == target_all[other], 1.0, 0.0).astype(jnp.bfloat16)
-            partial[...] += jnp.dot(placing, flux_all[other], preferred_element_type=F32)
-            return carry
-        lax.fori_loop(0, groups, add, 0)
-
-        def push(to_member, carry):
-            itself = is_self(to_member)
-            @pl.when(itself)
-            def _():
-                parts[member] = partial[pl.ds(pl.multiple_of(member * width, 8), window)]
-            @pl.when(jnp.logical_not(itself))
-            def _():
-                copy2(to_member, member).start()
-            return carry
-        lax.fori_loop(0, span, push, 0)
-
-    wall_ref[...] = jnp.zeros_like(wall_ref)
-
-    @pl.when(owner)
-    def _():
-        def add(other, carry):
-            @pl.when(jnp.logical_not(is_self(other)))
-            def _():
-                copy2(other, other).wait_recv()
-            wall_ref[...] += parts[other]
-            return carry
-        lax.fori_loop(0, span, add, 0)
-
-    @pl.when(depth < 2)
-    def _():
-        def drain(half, carry):
-            to_group = 2 * half + depth
-            @pl.when(to_group != group)
-            def _():
-                for copy in copies1(to_group, group):
-                    copy.wait_send()
-            return carry
-        lax.fori_loop(0, groups // 2, drain, 0)
-
-    @pl.when(collects)
-    def _():
-        def drain(to_member, carry):
-            @pl.when(jnp.logical_not(is_self(to_member)))
-            def _():
-                copy2(to_member, member).wait_send()
-            return carry
-        lax.fori_loop(0, span, drain, 0)
+                self.parts[self.member] = self.rows_for(self.member)[...]
+            self.each_member(lambda copy: copy.start())
+
+    def add_to(self, source, row):
+        @pl.when(self.owner)
+        def _():
+            def body(other, carry):
+                @pl.when(jnp.logical_not(self.is_self(other)))
+                def _():
+                    self.copy2(other, other).wait_recv()
+                source[row] = source[row] + self.parts[other]
+                return carry
+            lax.fori_loop(0, self.span, body, 0)
+
+    def finish(self):
+        self.each_group(lambda copy: copy.wait_send())
+
+        @pl.when(self.collects)
+        def _():
+            self.each_member(lambda copy: copy.wait_send())
 
 
 SIDES = [(dz, dx) for dz in (-1, 0, 1) for dx in (-1, 0, 1) if (dz, dx) != (0, 0)]
@@ -193,8 +182,9 @@
         level.U[2 + 2 * row] = level.U[2 + 2 * row] + wide
 
 
-def cycles_kernel(n_surf, n_depth, n_zones,
-                  temp_ref, virgin_ref, zone_ref, props_ref, wall_ref, out_ref,
+def cycles_kernel(n_surf, n_depth, n_zones, groups, span,
+                  temp_hbm, virgin_hbm, zone_hbm, props_hbm, flux_hbm, owner_hbm, cell_hbm, out_ref,
+                  temp_ref, virgin_ref, zone_ref, props_ref, owner_ref, cell_ref, in_sem, wall_refs,
                   packed, guess, temp, virgin,
                   fd0, fx0, fy0, fz0, fd1, fx1, fy1, fz1, fd2, fx2, fy2, fz2, fd3, fx3, fy3, fz3,
                   l0, l1, l2, res, t0, t1, t2, v1, v2, b3,
@@ -209,6 +199,17 @@
     levels = [Level(refs, 8 >> index, 8 >> index) for index, refs in enumerate((l0, l1, l2))]
     top, mid, low = levels
 
+    width = out_ref.shape[1]
+    wall = Wall(groups, span, width, wall_refs)
+    inputs = [
+        pltpu.make_async_copy(src, dst, in_sem.at[index])
+        for index, (src, dst) in enumerate((
+            (temp_hbm, temp_ref), (virgin_hbm, virgin_ref), (zone_hbm.at[0], zone_ref), (flux_hbm, wall.flux),
+            (owner_hbm, owner_ref), (cell_hbm, cell_ref), (props_hbm, props_ref)))
+    ]
+    for copy in inputs:
+        copy.start()
+
     barrier = pltpu.get_barrier_semaphore()
 
     def greet(dz, carry):
@@ -219,14 +220,18 @@
     for dx in (-1, 1):
         pl.semaphore_signal(barrier, inc=1, device_id=at(0, dx), device_id_type=MESH)
     lax.fori_loop(1, n_depth, greet, 0)
+    wall.greet(barrier)
+    for copy in inputs:
+        copy.wait()
+    wall.target[...] = owner_ref[...] * width + cell_ref[...]
 
     own_t = temp_ref[...]
     own_v = virgin_ref[...]
     code_t = ((own_t - 0.5) * (65535.0 / 1.5) + 0.5).astype(jnp.int32)
     code_v = ((own_v - 0.2) * (65535.0 / 0.8) + 0.5).astype(jnp.int32)
     packed[1, 0:8, 8:24] = jnp.left_shift(code_t, 16) | code_v
-    packed[1, 8, 8:24] = zone_ref[0]
-    pl.semaphore_wait(barrier, 3 * n_depth - 1)
+    packed[1, 8, 8:24] = zone_ref[...]
+    pl.semaphore_wait(barrier, 3 * n_depth - 1 + wall.greetings())
 
     src_x = {-1: (8, 8), 0: (8, 16), 1: (16, 8)}
     dst_x = {-1: 24, 0: 8, 1: 0}
@@ -252,6 +257,7 @@
             guess.at[pl.ds(1 + 8 * (1 - dz) + low_row, rows), pl.ds(dst_x[dx], count)],
             e_send, e_recv, dz, dx)
 
+    wall.each_group(lambda copy: copy.start())
     for index in range(8):
         setup_copy(index).start()
 
@@ -275,6 +281,8 @@
     guess[25] = jnp.zeros(guess.shape[1:], F32)
     solved[0] = jnp.zeros(solved.shape[1:], F32)
     solved[n_depth + 1] = jnp.zeros(solved.shape[1:], F32)
+
+    wall.collect()
 
     for index in range(8):
         setup_copy(index).wait_recv()
@@ -378,9 +386,7 @@
     each_column(0, lambda copy: copy.start())
     coef_all[depth, :, 1:3] = coef_own[...]
 
-    @pl.when(depth == 0)
-    def _():
-        top.B[8] = top.B[8] + wall_ref[...]
+    wall.add_to(top.B, 8)
 
     def down(level, scratch, coarse_rhs, chunk):
         for row in range(0, level.rows, chunk):
@@ -503,6 +509,7 @@
     for index in range(8):
         setup_copy(index).wait_send()
         guess_copy(index).wait_send()
+    wall.finish()
     for phase in range(3):
         each_column(phase, lambda copy: copy.wait_send())
     for cycle in range(2):
@@ -514,27 +521,8 @@
     width = temp_old.shape[1]
     span = min(GROUP, n_surf // 2)
     groups = n_surf // span
-    vmem = pl.BlockSpec(memory_space=pltpu.VMEM)
-    smem = pl.BlockSpec(memory_space=pltpu.SMEM)
+    rows = gas_flux.shape[0]
     dma = pltpu.SemaphoreType.DMA
-    rows = gas_flux.shape[0]
-    target = (gas_owner[:, 0] * width + gas_cell).reshape(1, rows)
-
-    wall = pl.pallas_call(
-        functools.partial(gas_kernel, groups, width, span),
-        out_shape=jax.ShapeDtypeStruct((2 * width, LANES), F32),
-        in_specs=[vmem, vmem],
-        out_specs=vmem,
-        scratch_shapes=[
-            pltpu.VMEM((groups, rows, LANES), jnp.bfloat16),
-            pltpu.VMEM((groups, 1, rows), jnp.int32),
-            pltpu.VMEM((span * width + width, LANES), F32),
-            pltpu.VMEM((span, 2 * width, LANES), F32),
-            dma((2, groups)), dma((2, groups)), dma((span,)), dma((span,)),
-        ],
-        compiler_params=pltpu.CompilerParams(collective_id=0, has_side_effects=True),
-        name="wall",
-    )(gas_flux, target)
 
     def box(*shape):
         return pltpu.VMEM((*shape, LANES), F32)
@@ -547,7 +535,18 @@
         r, c = 24 >> index, 32 >> index
         return [box(r, c)] * 5 + [box(r + 2, c)] * 2
 
+    def ints(*shape):
+        return pltpu.VMEM((*shape, LANES), jnp.int32)
+
+    wall = [
+        pltpu.VMEM((rows, LANES), jnp.bfloat16), ints(1),
+        pltpu.VMEM((groups, rows, LANES), jnp.bfloat16), ints(groups, 1),
+        box(span * width + width), box(span, 2 * width),
+        dma((2, groups)), dma((2, groups)), dma((span,)), dma((span,)),
+    ]
     scratch = [
+        box(*temp_old.shape[:2]), box(*temp_old.shape[:2]), ints(width), pltpu.SMEM(zone_props.shape, F32),
+        ints(1), ints(1), dma((7,)), wall,
         pltpu.VMEM((3, 9, 32, LANES), jnp.int32), box(26, 32), box(24, 32), box(24, 32),
         *fields(0), *fields(1), *fields(2), *fields(3),
         level(0), level(1), level(2),
@@ -559,15 +558,15 @@
         dma((3, n_depth, 3)), dma((3, n_depth, 3)), dma((2, 4)), dma((2, 4)),
     ]
     return pl.pallas_call(
-        functools.partial(cycles_kernel, n_surf, n_depth, zone_props.shape[1]),
+        functools.partial(cycles_kernel, n_surf, n_depth, zone_props.shape[1], groups, span),
         out_shape=jax.ShapeDtypeStruct(temp_old.shape, F32),
-        in_specs=[vmem, vmem, vmem, smem, vmem],
-        out_specs=vmem,
+        in_specs=[pl.BlockSpec(memory_space=pltpu.HBM)] * 7,
+        out_specs=pl.BlockSpec(memory_space=pltpu.VMEM),
         scratch_shapes=scratch,
         compiler_params=pltpu.CompilerParams(
-            collective_id=1, has_side_effects=True, vmem_limit_bytes=48 * 1024 * 1024),
+            collective_id=0, has_side_effects=True, vmem_limit_bytes=60 * 1024 * 1024),
         name="cycles",
-    )(temp_old, virgin, zone, zone_props, wall)
+    )(temp_old, virgin, zone, zone_props, gas_flux, gas_owner.reshape(1, rows), gas_cell.reshape(1, rows))
 
 
 def solution(mesh):

time: 87.3 us -> 75.2 us (0.86)
  the two profiles are of different devices: /device:TPU:9 before, /device:TPU:1 now
where the time goes in v2:
time: 75.2 us; the launch traced here: 75 us
  Pallas kernels  73.5 us (98%)
  local copies, waits for them, and re-layouts  1.47 us (2%)
    pallas_call x1, Pallas kernels, per_device(): pl.pallas_call(functools.partial(cycles_kernel, n_surf, n_depth, zone_pro...  73.5 us

profile of v2, /device:TPU:1, one launch (start us, length us, event | category | flops | bytes accessed | tf_op | source)
XLA Modules:
  0.0 75.0 jit_solution(14956156575649111052)
XLA Ops:
  0.0 73.5 %cycles.1 = f32[8,16,128]{2,1,0:T(8,128)} custom-call(f32[8,16,128]{2,1,0:T(8,128)} %temp_hbm.1, f32[8,16,128]{2,1,0:T(8,128)} %virgin_hbm.1, s32[8,16,128]{2,1,0:T(8,128)} %zone_hbm.1, f32[4,8]{1,0:T(4,128)} %props_hbm.1, bf16[128,128]{1,0:T(8,128)(2,1)} %flux_hbm.1, s32[1,128]{1,0:T(1,128)} %bitcast.2, s32[1,128]{1,0:T(1,128)} %bitcast.3), custom_call_target="tpu_custom_call" | custom-call | tf_op jit(solution)/shard_map/cycles/pallas_call | solution.py:560
  73.5 1.5 %copy.9 = f32[8,16,128]{2,1,0:T(8,128)} copy(f32[8,16,128]{2,1,0:T(8,128)} %cycles.1) | data formatting | bytes 131072

commit v3 on v2

--- a/solution.py
+++ b/solution.py
@@ -140,7 +140,7 @@
             self.each_member(lambda copy: copy.wait_send())
 
 
-SIDES = [(dz, dx) for dz in (-1, 0, 1) for dx in (-1, 0, 1) if (dz, dx) != (0, 0)]
+SIDES = [(-1, 0), (1, 0), (-1, -1), (-1, 1), (1, -1), (1, 1), (0, -1), (0, 1)]
 
 
 class Level:
@@ -209,17 +209,22 @@
     ]
     for copy in inputs:
         copy.start()
+    for columns in (pl.ds(0, 8), pl.ds(24, 8)):
+        for block in (0, 2):
+            packed[block, :, columns] = jnp.zeros((10, 8, LANES), jnp.int32)
+            guess[pl.ds(1 + 8 * block, 8), columns] = jnp.zeros((8, 8, LANES), F32)
 
     barrier = pltpu.get_barrier_semaphore()
 
-    def greet(dz, carry):
+    def greet(step, carry):
+        dz = n_depth // 2 + jnp.where(lax.rem(step, 2) == 1, (step + 1) // 2, -(step // 2))
         for dx in (-1, 0, 1):
             pl.semaphore_signal(barrier, inc=1, device_id=at(dz, dx), device_id_type=MESH)
         return carry
 
+    lax.fori_loop(0, n_depth - 1, greet, 0)
     for dx in (-1, 1):
         pl.semaphore_signal(barrier, inc=1, device_id=at(0, dx), device_id_type=MESH)
-    lax.fori_loop(1, n_depth, greet, 0)
     wall.greet(barrier)
     for copy in inputs:
         copy.wait()
@@ -229,8 +234,9 @@
     own_v = virgin_ref[...]
     code_t = ((own_t - 0.5) * (65535.0 / 1.5) + 0.5).astype(jnp.int32)
     code_v = ((own_v - 0.2) * (65535.0 / 0.8) + 0.5).astype(jnp.int32)
-    packed[1, 0:8, 8:24] = jnp.left_shift(code_t, 16) | code_v
-    packed[1, 8, 8:24] = zone_ref[...]
+    packed[1, 1:9, 8:24] = jnp.left_shift(code_t, 16) | code_v
+    packed[1, 0, 8:24] = zone_ref[...]
+    packed[1, 9, 8:24] = zone_ref[...]
     pl.semaphore_wait(barrier, 3 * n_depth - 1 + wall.greetings())
 
     src_x = {-1: (8, 8), 0: (8, 16), 1: (16, 8)}
@@ -241,25 +247,48 @@
             src_ref=ref_src, dst_ref=ref_dst, send_sem=send.at[index], recv_sem=recv.at[index],
             device_id=at(dz, dx), device_id_type=MESH)
 
-    def setup_copy(index):
-        dz, dx = SIDES[index]
-        first, count = src_x[dx]
-        return ring_copy(
-            index, packed.at[1, :, pl.ds(first, count)],
-            packed.at[1 - dz, :, pl.ds(dst_x[dx], count)], s_send, s_recv, dz, dx)
-
-    def guess_copy(index):
-        dz, dx = SIDES[index]
-        first, count = src_x[dx]
-        low_row, rows = (0, 8) if dx == 0 or dz == 0 else ((0, 7) if dz < 0 else (1, 7))
-        return ring_copy(
-            index, guess.at[pl.ds(9 + low_row, rows), pl.ds(first, count)],
-            guess.at[pl.ds(1 + 8 * (1 - dz) + low_row, rows), pl.ds(dst_x[dx], count)],
-            e_send, e_recv, dz, dx)
-
+    def pieces(sizes, dz, dx):
+        found = []
+        for first_row, last_row, columns in sizes:
+            first = first_row if dz < 0 else 9 - last_row
+            count = last_row - first_row + 1
+            low, _ = src_x[dx]
+            skip = 0 if dx < 0 else 8 - columns
+            found.append((first, count, low + skip, dst_x[dx] + skip, columns))
+        return found
+
+    def setup_copies():
+        copies = []
+        for dz, dx in SIDES:
+            if dz and dx:
+                near, far = pieces(((1, 4, 8), (5, 8, 4)), dz, dx)
+                near = (near[0] - (1 if dz < 0 else 0), near[1] + 1) + near[2:]
+                parts = [near, far]
+            else:
+                parts = [(1 if dz > 0 else 0, 9, src_x[dx][0], dst_x[dx], src_x[dx][1])]
+            for row, rows, src, dst, columns in parts:
+                copies.append(((dz, dx), ring_copy(
+                    len(copies), packed.at[1, pl.ds(row, rows), pl.ds(src, columns)],
+                    packed.at[1 - dz, pl.ds(row, rows), pl.ds(dst, columns)], s_send, s_recv, dz, dx)))
+        return copies
+
+    def guess_copies():
+        copies = []
+        for dz, dx in SIDES:
+            if dz and dx:
+                parts = pieces(((1, 3, 7), (4, 7, 4)), dz, dx)
+            else:
+                parts = [(1, 8, src_x[dx][0], dst_x[dx], src_x[dx][1])]
+            for row, rows, src, dst, columns in parts:
+                copies.append(ring_copy(
+                    len(copies), guess.at[pl.ds(8 + row, rows), pl.ds(src, columns)],
+                    guess.at[pl.ds(8 * (1 - dz) + row, rows), pl.ds(dst, columns)], e_send, e_recv, dz, dx))
+        return copies
+
+    ring_inputs, ring_guess = setup_copies(), guess_copies()
     wall.each_group(lambda copy: copy.start())
-    for index in range(8):
-        setup_copy(index).start()
+    for _, copy in ring_inputs:
+        copy.start()
 
     def column_mask(level):
         column = lax.broadcasted_iota(jnp.int32, (level.cols, LANES), 0)
@@ -284,17 +313,18 @@
 
     wall.collect()
 
-    for index in range(8):
-        setup_copy(index).wait_recv()
-    for block in range(3):
-        code = packed[block, 0:8]
+    for block in (1, 0, 2):
+        for (dz, _), copy in ring_inputs:
+            if dz == 1 - block:
+                copy.wait_recv()
+        code = packed[block, 1:9]
         rows = pl.ds(8 * block, 8)
         temp[rows] = 0.5 + lax.shift_right_logical(code, 16).astype(F32) * (1.5 / 65535.0)
         virgin[rows] = 0.2 + (code & 0xFFFF).astype(F32) * (0.8 / 65535.0)
-    temp[8:16, 8:24] = own_t
-    virgin[8:16, 8:24] = own_v
-    for block in range(3):
-        zone = packed[block, 8]
+        if block == 1:
+            temp[rows, 8:24] = own_t
+            virgin[rows, 8:24] = own_v
+        zone = packed[block, 9 if block == 0 else 0]
         inside = masks[0] * row_mask[block]
         props = [jnp.zeros((top.cols, LANES), F32) for _ in range(4)]
         for number in range(n_zones):
@@ -487,13 +517,10 @@
 
     top.U[1:25] = top.WI[...] * top.B[...]
     run_cycle(0, False)
-    for index in range(8):
-        guess_copy(index).start()
-    for index in range(8):
-        guess_copy(index).wait_recv()
-    for rows in (pl.ds(1, 1), pl.ds(24, 1)):
-        for columns in (pl.ds(0, 8), pl.ds(24, 8)):
-            guess[rows, columns] = jnp.zeros((1, 8, LANES), F32)
+    for copy in ring_guess:
+        copy.start()
+    for copy in ring_guess:
+        copy.wait_recv()
     for block in range(3):
         rows = pl.ds(1 + 8 * block, 8)
         if block == 1:
@@ -506,9 +533,8 @@
         top.U[padded] = guess[padded] + top.WI[rows] * residual(top, guess, row, 4)
     run_cycle(1, True)
 
-    for index in range(8):
-        setup_copy(index).wait_send()
-        guess_copy(index).wait_send()
+    for copy in [copy for _, copy in ring_inputs] + ring_guess:
+        copy.wait_send()
     wall.finish()
     for phase in range(3):
         each_column(phase, lambda copy: copy.wait_send())
@@ -547,14 +573,14 @@
     scratch = [
         box(*temp_old.shape[:2]), box(*temp_old.shape[:2]), ints(width), pltpu.SMEM(zone_props.shape, F32),
         ints(1), ints(1), dma((7,)), wall,
-        pltpu.VMEM((3, 9, 32, LANES), jnp.int32), box(26, 32), box(24, 32), box(24, 32),
+        pltpu.VMEM((3, 10, 32, LANES), jnp.int32), box(26, 32), box(24, 32), box(24, 32),
         *fields(0), *fields(1), *fields(2), *fields(3),
         level(0), level(1), level(2),
         box(24, 32), box(12, 32), box(6, 16), box(3, 8), box(12, 16), box(6, 8), box(3, 4),
         box(2, 2, 1), box(n_depth, 2, 4, 1), box(2, 2, 1), box(2, n_depth, 4, 1),
         box(n_depth, 4, 1), box(n_depth, 4, 1), box(n_depth + 2, 4, 1), box(3, 8),
         box(2, 2, 2, 8), box(2, 2, 2, 8), box(2, 2, 4, 1), box(2, 2, 4, 1),
-        dma((8,)), dma((8,)), dma((8,)), dma((8,)),
+        dma((12,)), dma((12,)), dma((12,)), dma((12,)),
         dma((3, n_depth, 3)), dma((3, n_depth, 3)), dma((2, 4)), dma((2, 4)),
     ]
     return pl.pallas_call(
@@ -564,9 +590,9 @@
         out_specs=pl.BlockSpec(memory_space=pltpu.VMEM),
         scratch_shapes=scratch,
         compiler_params=pltpu.CompilerParams(
-            collective_id=0, has_side_effects=True, vmem_limit_bytes=60 * 1024 * 1024),
+            collective_id=0, has_side_effects=True, vmem_limit_bytes=48 * 1024 * 1024),
         name="cycles",
-    )(temp_old, virgin, zone, zone_props, gas_flux, gas_owner.reshape(1, rows), gas_cell.reshape(1, rows))
+    )(*[pltpu.with_memory_space_constraint(a, pltpu.HBM) for a in (temp_old, virgin, zone, zone_props, gas_flux, gas_owner.reshape(1, rows), gas_cell.reshape(1, rows))])
 
 
 def solution(mesh):

time: 75.2 us -> 70.6 us (0.939)
  Pallas kernels: 73.5 us -> 69.8 us
  local copies, waits for them, and re-layouts: 1.47 us -> 0.63 us
    pallas_call x1, Pallas kernels: 73.5 us -> 69.8 us  [per_device(): pl.pallas_call(functools.partial(cycles_kernel, n_surf, n_depth, zone_pro...]
    unnamed x1, local copies, waits for them, and re-layouts: 1.47 us -> 0.63 us
where the time goes in v3:
time: 70.6 us; the launch traced here: 70.4 us
  Pallas kernels  69.8 us (99%)
    pallas_call x1, Pallas kernels, per_device(): pl.pallas_call(functools.partial(cycles_kernel, n_surf, n_depth, zone_pro...  69.8 us

profile of v3, /device:TPU:1, one launch (start us, length us, event | category | flops | bytes accessed | tf_op | source)
XLA Modules:
  0.0 70.4 jit_solution(15810170909700335873)
XLA Ops:
  0.0 69.8 %cycles.1 = f32[8,16,128]{2,1,0:T(8,128)S(1)} custom-call(f32[8,16,128]{2,1,0:T(8,128)} %temp_hbm.1, f32[8,16,128]{2,1,0:T(8,128)} %virgin_hbm.1, s32[8,16,128]{2,1,0:T(8,128)} %zone_hbm.1, f32[4,8]{1,0:T(4,128)} %props_hbm.1, bf16[128,128]{1,0:T(8,128)(2,1)} %flux_hbm.1, s32[1,128]{1,0:T(1,128)} %bitcast.2, s32[1,128]{1,0:T(1,128)} %bitcast.3), custom_call_target="tpu_custom_call" | custom-call | tf_op jit(solution)/shard_map/cycles/pallas_call | solution.py:586
  69.8 0.6 copy.9

commit v4 on v3

--- a/solution.py
+++ b/solution.py
@@ -185,7 +185,7 @@
 def cycles_kernel(n_surf, n_depth, n_zones, groups, span,
                   temp_hbm, virgin_hbm, zone_hbm, props_hbm, flux_hbm, owner_hbm, cell_hbm, out_ref,
                   temp_ref, virgin_ref, zone_ref, props_ref, owner_ref, cell_ref, in_sem, wall_refs,
-                  packed, guess, temp, virgin,
+                  packed, zones, guess, temp, virgin,
                   fd0, fx0, fy0, fz0, fd1, fx1, fy1, fz1, fd2, fx2, fy2, fz2, fd3, fx3, fy3, fz3,
                   l0, l1, l2, res, t0, t1, t2, v1, v2, b3,
                   coef_own, coef_all, rhs_own, rhs_all, ratio, inverse, solved, e2,
@@ -211,7 +211,7 @@
         copy.start()
     for columns in (pl.ds(0, 8), pl.ds(24, 8)):
         for block in (0, 2):
-            packed[block, :, columns] = jnp.zeros((10, 8, LANES), jnp.int32)
+            packed[block, :, columns] = jnp.zeros((8, 8, LANES), jnp.int32)
             guess[pl.ds(1 + 8 * block, 8), columns] = jnp.zeros((8, 8, LANES), F32)
 
     barrier = pltpu.get_barrier_semaphore()
@@ -234,9 +234,9 @@
     own_v = virgin_ref[...]
     code_t = ((own_t - 0.5) * (65535.0 / 1.5) + 0.5).astype(jnp.int32)
     code_v = ((own_v - 0.2) * (65535.0 / 0.8) + 0.5).astype(jnp.int32)
-    packed[1, 1:9, 8:24] = jnp.left_shift(code_t, 16) | code_v
-    packed[1, 0, 8:24] = zone_ref[...]
-    packed[1, 9, 8:24] = zone_ref[...]
+    packed[1, :, 8:24] = jnp.left_shift(code_t, 16) | code_v
+    for half in range(2):
+        zones[1, 1 + half] = zone_ref[8 * half : 8 * half + 1]
     pl.semaphore_wait(barrier, 3 * n_depth - 1 + wall.greetings())
 
     src_x = {-1: (8, 8), 0: (8, 16), 1: (16, 8)}
@@ -261,22 +261,24 @@
         copies = []
         for dz, dx in SIDES:
             if dz and dx:
-                near, far = pieces(((1, 4, 8), (5, 8, 4)), dz, dx)
-                near = (near[0] - (1 if dz < 0 else 0), near[1] + 1) + near[2:]
-                parts = [near, far]
+                parts = pieces(((1, 4, 8), (5, 8, 4)), dz, dx)
             else:
-                parts = [(1 if dz > 0 else 0, 9, src_x[dx][0], dst_x[dx], src_x[dx][1])]
+                parts = [(1, 8, src_x[dx][0], dst_x[dx], src_x[dx][1])]
             for row, rows, src, dst, columns in parts:
                 copies.append(((dz, dx), ring_copy(
-                    len(copies), packed.at[1, pl.ds(row, rows), pl.ds(src, columns)],
-                    packed.at[1 - dz, pl.ds(row, rows), pl.ds(dst, columns)], s_send, s_recv, dz, dx)))
+                    len(copies), packed.at[1, pl.ds(row - 1, rows), pl.ds(src, columns)],
+                    packed.at[1 - dz, pl.ds(row - 1, rows), pl.ds(dst, columns)], s_send, s_recv, dz, dx)))
+            src, count, dst = {-1: (1, 1, 3), 0: (1, 2, 1), 1: (2, 1, 0)}[dx]
+            copies.append(((dz, dx), ring_copy(
+                len(copies), zones.at[1, pl.ds(src, count)], zones.at[1 - dz, pl.ds(dst, count)],
+                s_send, s_recv, dz, dx)))
         return copies
 
     def guess_copies():
         copies = []
         for dz, dx in SIDES:
             if dz and dx:
-                parts = pieces(((1, 3, 7), (4, 7, 4)), dz, dx)
+                parts = pieces(((1, 2, 7), (3, 4, 5), (5, 7, 3)), dz, dx)
             else:
                 parts = [(1, 8, src_x[dx][0], dst_x[dx], src_x[dx][1])]
             for row, rows, src, dst, columns in parts:
@@ -317,14 +319,14 @@
         for (dz, _), copy in ring_inputs:
             if dz == 1 - block:
                 copy.wait_recv()
-        code = packed[block, 1:9]
+        code = packed[block]
         rows = pl.ds(8 * block, 8)
         temp[rows] = 0.5 + lax.shift_right_logical(code, 16).astype(F32) * (1.5 / 65535.0)
         virgin[rows] = 0.2 + (code & 0xFFFF).astype(F32) * (0.8 / 65535.0)
         if block == 1:
             temp[rows, 8:24] = own_t
             virgin[rows, 8:24] = own_v
-        zone = packed[block, 9 if block == 0 else 0]
+        zone = jnp.concatenate([jnp.broadcast_to(zones[block, part], (8, LANES)) for part in range(4)], axis=0)
         inside = masks[0] * row_mask[block]
         props = [jnp.zeros((top.cols, LANES), F32) for _ in range(4)]
         for number in range(n_zones):
@@ -454,6 +456,18 @@
         for copy in near:
             copy.start()
         rhs_all[cycle, depth, 1:3] = rhs_own[cycle]
+
+        if cycle == 0:
+            for _, copy in ring_inputs:
+                copy.wait_send()
+            each_column(0, lambda copy: copy.wait_send())
+            wall.finish()
+        else:
+            for copy in ring_guess:
+                copy.wait_send()
+            each_column(1, lambda copy: copy.wait_send())
+            for copy in near_copies(0):
+                copy.wait_send()
 
         if cycle == 0:
             each_column(0, lambda copy: copy.wait_recv())
@@ -533,14 +547,9 @@
         top.U[padded] = guess[padded] + top.WI[rows] * residual(top, guess, row, 4)
     run_cycle(1, True)
 
-    for copy in [copy for _, copy in ring_inputs] + ring_guess:
+    each_column(2, lambda copy: copy.wait_send())
+    for copy in near_copies(1):
         copy.wait_send()
-    wall.finish()
-    for phase in range(3):
-        each_column(phase, lambda copy: copy.wait_send())
-    for cycle in range(2):
-        for copy in near_copies(cycle):
-            copy.wait_send()
 
 
 def per_device(n_surf, n_depth, temp_old, virgin, zone, zone_props, gas_flux, gas_owner, gas_cell):
@@ -573,14 +582,14 @@
     scratch = [
         box(*temp_old.shape[:2]), box(*temp_old.shape[:2]), ints(width), pltpu.SMEM(zone_props.shape, F32),
         ints(1), ints(1), dma((7,)), wall,
-        pltpu.VMEM((3, 10, 32, LANES), jnp.int32), box(26, 32), box(24, 32), box(24, 32),
+        pltpu.VMEM((3, 8, 32, LANES), jnp.int32), ints(3, 4, 1), box(26, 32), box(24, 32), box(24, 32),
         *fields(0), *fields(1), *fields(2), *fields(3),
         level(0), level(1), level(2),
         box(24, 32), box(12, 32), box(6, 16), box(3, 8), box(12, 16), box(6, 8), box(3, 4),
         box(2, 2, 1), box(n_depth, 2, 4, 1), box(2, 2, 1), box(2, n_depth, 4, 1),
         box(n_depth, 4, 1), box(n_depth, 4, 1), box(n_depth + 2, 4, 1), box(3, 8),
         box(2, 2, 2, 8), box(2, 2, 2, 8), box(2, 2, 4, 1), box(2, 2, 4, 1),
-        dma((12,)), dma((12,)), dma((12,)), dma((12,)),
+        dma((20,)), dma((20,)), dma((16,)), dma((16,)),
         dma((3, n_depth, 3)), dma((3, n_depth, 3)), dma((2, 4)), dma((2, 4)),
     ]
     return pl.pallas_call(

time: 70.6 us -> 69.4 us (0.983)
  Pallas kernels: 69.8 us -> 68.6 us
    pallas_call x1, Pallas kernels: 69.8 us -> 68.6 us  [per_device(): pl.pallas_call(functools.partial(cycles_kernel, n_surf, n_depth, zone_pro...]
where the time goes in v4:
time: 69.4 us; the launch traced here: 69.2 us
  Pallas kernels  68.6 us (99%)
    pallas_call x1, Pallas kernels, per_device(): pl.pallas_call(functools.partial(cycles_kernel, n_surf, n_depth, zone_pro...  68.6 us

profile of v4, /device:TPU:1, one launch (start us, length us, event | category | flops | bytes accessed | tf_op | source)
XLA Modules:
  0.0 69.2 jit_solution(1665330943245931997)
XLA Ops:
  0.0 68.6 %cycles.1 = f32[8,16,128]{2,1,0:T(8,128)S(1)} custom-call(f32[8,16,128]{2,1,0:T(8,128)} %temp_hbm.1, f32[8,16,128]{2,1,0:T(8,128)} %virgin_hbm.1, s32[8,16,128]{2,1,0:T(8,128)} %zone_hbm.1, f32[4,8]{1,0:T(4,128)} %props_hbm.1, bf16[128,128]{1,0:T(8,128)(2,1)} %flux_hbm.1, s32[1,128]{1,0:T(1,128)} %bitcast.2, s32[1,128]{1,0:T(1,128)} %bitcast.3), custom_call_target="tpu_custom_call" | custom-call | tf_op jit(solution)/shard_map/cycles/pallas_call | solution.py:595
  68.6 0.6 copy.9

commit v5 on v4

--- a/solution.py
+++ b/solution.py
@@ -310,6 +310,8 @@
         ref[ref.shape[0] - 1] = jnp.zeros(ref.shape[1:], F32)
     guess[0] = jnp.zeros(guess.shape[1:], F32)
     guess[25] = jnp.zeros(guess.shape[1:], F32)
+    for row in (0, 1, 22, 23):
+        res[row] = jnp.zeros(res.shape[1:], F32)
     solved[0] = jnp.zeros(solved.shape[1:], F32)
     solved[n_depth + 1] = jnp.zeros(solved.shape[1:], F32)
 
@@ -421,7 +423,8 @@
     wall.add_to(top.B, 8)
 
     def down(level, scratch, coarse_rhs, chunk):
-        for row in range(0, level.rows, chunk):
+        edge = 2 if level is top else 0
+        for row in range(edge, level.rows - edge, chunk):
             res[pl.ds(row, chunk), 0 : level.cols] = residual(level, level.U, row, chunk)
         restrict_into(res.at[:, pl.ds(0, level.cols)], 0, scratch, coarse_rhs, 0)
 

time: 69.4 us -> 69.1 us (level)
  no operation moved by 1% of the time
where the time goes in v5:
time: 69.1 us; the launch traced here: 69 us
  Pallas kernels  68.3 us (99%)
    pallas_call x1, Pallas kernels, per_device(): pl.pallas_call(functools.partial(cycles_kernel, n_surf, n_depth, zone_pro...  68.3 us

profile of v5, /device:TPU:1, one launch (start us, length us, event | category | flops | bytes accessed | tf_op | source)
XLA Modules:
  0.0 69.0 jit_solution(9084492572162973501)
XLA Ops:
  0.0 68.3 %cycles.1 = f32[8,16,128]{2,1,0:T(8,128)S(1)} custom-call(f32[8,16,128]{2,1,0:T(8,128)} %temp_hbm.1, f32[8,16,128]{2,1,0:T(8,128)} %virgin_hbm.1, s32[8,16,128]{2,1,0:T(8,128)} %zone_hbm.1, f32[4,8]{1,0:T(4,128)} %props_hbm.1, bf16[128,128]{1,0:T(8,128)(2,1)} %flux_hbm.1, s32[1,128]{1,0:T(1,128)} %bitcast.2, s32[1,128]{1,0:T(1,128)} %bitcast.3), custom_call_target="tpu_custom_call" | custom-call | tf_op jit(solution)/shard_map/cycles/pallas_call | solution.py:598
  68.3 0.6 copy.9
